TPU v7x, 256 devices: a whole 4x4x8 slice. The times are simulated.
256 devices in a mesh: dp: 4 (over x), ep: 64 (over y, z, core).
Axes of the slice: x: 4, y: 4, z: 8, core: 2. Of those that a mesh axis runs over, the one named last changes fastest.
Arguments:
- tokens: bfloat16 [4, 2048, 2048], P('dp', 'ep'), may hold values from -12 to 12
- cotangent: bfloat16 [4, 2048, 2048], P('dp', 'ep'), may hold values from -6 to 6
- assign: int32 [4, 2048, 8], P('dp', 'ep'), may hold values from 0 to 63, as said below
- w_router: bfloat16 [2048, 64], replicated, may hold values from -0.125 to 0.125
- w_gate: bfloat16 [64, 2048, 768], P('ep'), may hold values from -0.125 to 0.125
- w_up: bfloat16 [64, 2048, 768], P('ep'), may hold values from -0.125 to 0.125
- w_down: bfloat16 [64, 2048, 768], P('ep'), may hold values from -0.21875 to 0.21875
Outputs:
- grad_tokens: bfloat16 [4, 2048, 2048], P('dp', 'ep')
- grad_router: float32 [2048, 64], replicated
- grad_gate: bfloat16 [64, 2048, 768], P('ep', 'dp')
- grad_up: bfloat16 [64, 2048, 768], P('ep', 'dp')
- grad_down: bfloat16 [64, 2048, 768], P('ep', 'dp')
Inputs may be any that keep to these rules, and one draw needn't show every extreme that they name: `assign`: each token names 8 different experts; the routes of the 32 tokens of one device name one expert at most 8 times, and in every draw one expert is named exactly 8 times by the routes of every device.
All inputs are finite; a program needn't handle non-finite values.
Results may differ from a plain program's by a relative error of at most 0.015.
Values may be sent and summed in bfloat16 or wider, within the bound.
A program may use at most 128 MiB of HBM per device.

v0:
```python
import jax
import jax.numpy as jnp
from jax import lax
from jax.sharding import PartitionSpec as P

ITERS = 3
cos_scale = 48.0
eps_norm = 1e-06
contract_first = (((0,), (0,)), ((), ()))
contract_last = (((1,), (1,)), ((), ()))


def logit_map(flat_tokens, router):
    inner_products = jnp.dot(flat_tokens, router, precision=lax.Precision.HIGHEST)
    token_norm = jnp.sqrt(jnp.sum(flat_tokens * flat_tokens, axis=1) + eps_norm)
    column_norm = jnp.sqrt(jnp.sum(router * router, axis=0) + eps_norm)
    return cos_scale * inner_products / (token_norm[:, None] * column_norm[None, :])


def expert_backward(expert_rows, expert_cotangent, rows_gate, gate_matrix, up_matrix, down_matrix):
    gate_linear = jnp.dot(expert_rows, gate_matrix, preferred_element_type=jnp.float32)
    up_linear = jnp.dot(expert_rows, up_matrix, preferred_element_type=jnp.float32)
    sigmoid_gate = jax.nn.sigmoid(gate_linear)
    activation = gate_linear * sigmoid_gate
    product = activation * up_linear
    hidden = product.astype(jnp.bfloat16)
    weighted = (rows_gate[:, None] * product).astype(jnp.bfloat16)
    raw_back = jnp.dot(expert_cotangent, down_matrix, preferred_element_type=jnp.float32)
    gate_grad = jnp.sum(raw_back * hidden.astype(jnp.float32), axis=1).astype(jnp.bfloat16)
    scaled_back = rows_gate[:, None] * raw_back
    up_delta = (scaled_back * activation).astype(jnp.bfloat16)
    gate_delta = (
        scaled_back * up_linear * sigmoid_gate * (1.0 + gate_linear * (1.0 - sigmoid_gate))
    ).astype(jnp.bfloat16)
    route_back = (
        lax.dot_general(gate_delta, gate_matrix, contract_last, preferred_element_type=jnp.float32)
        + lax.dot_general(up_delta, up_matrix, contract_last, preferred_element_type=jnp.float32)
    ).astype(jnp.bfloat16)
    return (gate_grad, route_back, gate_delta, up_delta, weighted)


def column_sums(values):
    return lax.psum(jnp.sum(values, axis=0), "ep")


def per_device(tokens, cotangent, assign, w_router, w_gate, w_up, w_down):
    local_tokens = tokens[0]
    local_cotangent = cotangent[0]
    route_ids = assign[0]
    token_count, per_token = route_ids.shape
    model_width = local_tokens.shape[1]
    experts = w_router.shape[1]
    slot_cap = min(token_count, 2 * token_count * per_token // experts)
    logits, logit_vjp = jax.vjp(
        logit_map, local_tokens.astype(jnp.float32), w_router.astype(jnp.float32)
    )
    kernel_start = jnp.exp(logits)
    kernel = kernel_start
    saved_steps = []
    for sweep_index in range(ITERS):
        column = column_sums(kernel)
        scaled = kernel / column[None, :]
        row_total = jnp.sum(scaled, axis=1, keepdims=True)
        kernel = scaled / row_total
        saved_steps.append((column, scaled, row_total, kernel))
    expert_ids = jnp.arange(experts, dtype=jnp.int32)
    onehot = (route_ids[:, :, None] == expert_ids).astype(jnp.float32)
    picked = jnp.sum(onehot * kernel[:, None, :], axis=2)
    picked_sum = jnp.sum(picked, axis=1, keepdims=True)
    gates = picked / picked_sum
    gate_half = gates.astype(jnp.bfloat16)
    flat_route = route_ids.reshape(-1)
    member = (flat_route[:, None] == expert_ids).astype(jnp.int32)
    earlier = jnp.cumsum(member, axis=0) - member
    slot_index = jnp.sum(earlier * member, axis=1)
    target = flat_route * slot_cap + slot_index
    route_slots = (
        jnp.arange(experts * slot_cap, dtype=jnp.int32)[:, None] == target[None, :]
    ).astype(jnp.bfloat16)
    token_slots = jnp.sum(route_slots.reshape(experts * slot_cap, token_count, per_token), axis=2)
    send_tokens = jnp.dot(token_slots, local_tokens, preferred_element_type=jnp.float32).astype(
        jnp.bfloat16
    )
    send_cotangent = jnp.dot(
        token_slots, local_cotangent, preferred_element_type=jnp.float32
    ).astype(jnp.bfloat16)
    send_gate = jnp.dot(
        route_slots, gate_half.reshape(-1), preferred_element_type=jnp.float32
    ).astype(jnp.bfloat16)
    recv_tokens, recv_cotangent, recv_gate = (
        lax.all_to_all(
            send_tokens.reshape(experts, slot_cap, model_width),
            "ep",
            split_axis=0,
            concat_axis=0,
            tiled=True,
        ),
        lax.all_to_all(
            send_cotangent.reshape(experts, slot_cap, model_width),
            "ep",
            split_axis=0,
            concat_axis=0,
            tiled=True,
        ),
        lax.all_to_all(
            send_gate.reshape(experts, slot_cap), "ep", split_axis=0, concat_axis=0, tiled=True
        ),
    )
    expert_rows = recv_tokens.reshape(-1, model_width)
    expert_cotangent = recv_cotangent.reshape(-1, model_width)
    rows_gate = recv_gate.reshape(-1).astype(jnp.float32)
    gate_grad, route_back, gate_delta, up_delta, weighted = expert_backward(
        expert_rows, expert_cotangent, rows_gate, w_gate[0], w_up[0], w_down[0]
    )
    back_rows, back_gate = (
        lax.all_to_all(
            route_back.reshape(experts, slot_cap, model_width),
            "ep",
            split_axis=0,
            concat_axis=0,
            tiled=True,
        ),
        lax.all_to_all(
            gate_grad.reshape(experts, slot_cap), "ep", split_axis=0, concat_axis=0, tiled=True
        ),
    )
    expert_back = lax.dot_general(
        token_slots,
        back_rows.reshape(-1, model_width),
        contract_first,
        preferred_element_type=jnp.float32,
    )
    route_grad = lax.dot_general(
        route_slots, back_gate.reshape(-1), contract_first, preferred_element_type=jnp.float32
    ).reshape(token_count, per_token)
    hidden_units = gate_delta.shape[1]
    summed = lax.psum_scatter(
        jnp.concatenate(
            [
                lax.dot_general(
                    expert_rows, gate_delta, contract_first, preferred_element_type=jnp.float32
                ),
                lax.dot_general(
                    expert_rows, up_delta, contract_first, preferred_element_type=jnp.float32
                ),
                lax.dot_general(
                    expert_cotangent, weighted, contract_first, preferred_element_type=jnp.float32
                ),
            ],
            axis=1,
        ).astype(jnp.bfloat16),
        "dp",
        scatter_dimension=0,
        tiled=True,
    ).astype(jnp.float32)
    grad_gate = summed[:, :hidden_units]
    grad_up = summed[:, hidden_units : 2 * hidden_units]
    grad_down = summed[:, 2 * hidden_units :]
    picked_grad = (route_grad - jnp.sum(route_grad * gates, axis=1, keepdims=True)) / picked_sum
    kernel_grad = jnp.sum(onehot * picked_grad[:, :, None], axis=1)
    for sweep_index in reversed(range(ITERS)):
        column, scaled, row_total, kernel_step = saved_steps[sweep_index]
        scaled_grad = (
            kernel_grad - jnp.sum(kernel_grad * kernel_step, axis=1, keepdims=True)
        ) / row_total
        moment = lax.psum(jnp.sum(scaled_grad * scaled, axis=0), "ep")
        kernel_grad = (scaled_grad - moment[None, :]) / column[None, :]
    logit_grad = kernel_grad * kernel_start
    router_back, router_part = logit_vjp(logit_grad)
    grad_router = lax.psum(router_part, ("dp", "ep"))
    grad_tokens = (expert_back + router_back).astype(jnp.bfloat16)[None]
    return (
        grad_tokens,
        grad_router,
        grad_gate.astype(jnp.bfloat16)[None],
        grad_up.astype(jnp.bfloat16)[None],
        grad_down.astype(jnp.bfloat16)[None],
    )


def solution(mesh):
    return jax.shard_map(
        per_device,
        mesh=mesh,
        in_specs=(
            P("dp", "ep", None),
            P("dp", "ep", None),
            P("dp", "ep", None),
            P(),
            P("ep", None, None),
            P("ep", None, None),
            P("ep", None, None),
        ),
        out_specs=(
            P("dp", "ep", None),
            P(),
            P("ep", "dp", None),
            P("ep", "dp", None),
            P("ep", "dp", None),
        ),
        check_vma=False,
    )
```

profile of v0, /device:TPU:2, one launch (start us, length us, event | category | flops | bytes accessed | tf_op | source)
XLA Modules:
  0.0 1251.3 jit_solution(17761611733418999477)
XLA Ops:
  15.1 131.8 %psum.49 = f32[64]{0:T(128)S(1)} all-reduce(f32[64]{0:T(128)S(1)} %get-tuple-element.33), channel_id=1, replica_groups=mesh['dp'=4,'ep'=64] {'ep'}, use_global_device_ids=true, to_apply=%region_7.0 | all-reduce | flops 64 | bytes 512 | tf_op jit(solution)/shard_map/psum | solution.py:43
  147.1 124.1 %psum.50 = f32[64]{0:T(128)S(1)} all-reduce(f32[64]{0:T(128)S(1)} %fusion.67), channel_id=1, replica_groups=mesh['dp'=4,'ep'=64] {'ep'}, use_global_device_ids=true, to_apply=%region_10.0 | all-reduce | flops 64 | bytes 512 | tf_op jit(solution)/shard_map/psum | solution.py:43
  271.4 124.0 %psum.51 = f32[64]{0:T(128)S(1)} all-reduce(f32[64]{0:T(128)S(1)} %fusion.73), channel_id=1, replica_groups=mesh['dp'=4,'ep'=64] {'ep'}, use_global_device_ids=true, to_apply=%region_13.0 | all-reduce | flops 64 | bytes 512 | tf_op jit(solution)/shard_map/psum | solution.py:43
  398.9 4.6 all-to-all-start
  406.9 6.1 all-to-all-done
  413.0 5.6 all-to-all-start.2
  420.6 49.0 %all-to-all-done.2 = bf16[64,8,2048]{2,1,0:T(8,128)(2,1)} async-done(((bf16[64,8,2048]{2,1,0:T(8,128)(2,1)}), bf16[64,8,2048]{2,1,0:T(8,128)(2,1)}, u32[]{:S(2)}, u32[]{:S(2)}) %all-to-all-start.2) | async-done | bytes 2097184 | tf_op jit(solution)/shard_map/all_to_all | solution.py:91
  469.6 6.1 all-to-all-start.1
  476.1 5.5 fusion.6
  481.6 4.6 fusion.2
  486.2 40.5 %all-to-all-done.1 = bf16[64,8,2048]{2,1,0:T(8,128)(2,1)} async-done(((bf16[64,8,2048]{2,1,0:T(8,128)(2,1)}), bf16[64,8,2048]{2,1,0:T(8,128)(2,1)}, u32[]{:S(2)}, u32[]{:S(2)}) %all-to-all-start.1) | async-done | bytes 2097184 | tf_op jit(solution)/shard_map/all_to_all | solution.py:98
  526.7 4.6 convolution_convert_fusion
  531.4 4.0 multiply_reduce_fusion
  535.4 4.0 convolution_convert_fusion.1
  539.5 3.4 convolution_convert_fusion.2
  542.9 4.5 pad_maximum_fusion
  548.1 6.4 all-to-all-start.4
  554.5 3.3 fusion
  557.8 3.1 fusion.14
  563.5 7.7 all-to-all-start.3
  580.8 155.9 %psum.52 = f32[64]{0:T(128)} all-reduce(f32[64]{0:T(128)} %multiply_reduce_fusion.7), channel_id=1, replica_groups=mesh['dp'=4,'ep'=64] {'ep'}, use_global_device_ids=true, to_apply=%region_22.23 | all-reduce | flops 64 | bytes 512 | tf_op jit(solution)/shard_map/psum | solution.py:166
  739.6 124.5 %psum.53 = f32[64]{0:T(128)} all-reduce(f32[64]{0:T(128)} %get-tuple-element.31), channel_id=1, replica_groups=mesh['dp'=4,'ep'=64] {'ep'}, use_global_device_ids=true, to_apply=%region_25.26 | all-reduce | flops 64 | bytes 512 | tf_op jit(solution)/shard_map/psum | solution.py:166
  866.9 124.7 %psum.54 = f32[64]{0:T(128)} all-reduce(f32[64]{0:T(128)} %multiply_reduce_fusion.3), channel_id=1, replica_groups=mesh['dp'=4,'ep'=64] {'ep'}, use_global_device_ids=true, to_apply=%region_28.29 | all-reduce | flops 64 | bytes 512 | tf_op jit(solution)/shard_map/psum | solution.py:166
  1010.7 231.3 %all-reduce.2.cloned.1.call-done = f32[2048,64]{0,1:T(8,128)} async-done(((f32[2048,64]{0,1:T(8,128)}), f32[2048,64]{0,1:T(8,128)}) %all-reduce.2.cloned.1.call-update) | async-done | bytes 524304 | tf_op jit(solution)/shard_map/psum | solution.py:170
  (134 shorter events, 56.1 us)
Async XLA Ops:
  8.0 473.6 %copy-start = (bf16[1,2048,768]{2,1,0:T(8,128)(2,1)S(1)}, bf16[1,2048,768]{2,1,0:T(8,128)(2,1)}, u32[]{:S(2)}) copy-start(bf16[1,2048,768]{2,1,0:T(8,128)(2,1)} %param.11) | copy-start | bytes 9437188
  8.9 404.0 %copy-start.3 = (s32[1,32,8]{2,1,0:T(8,128)}, s32[1,32,8]{2,1,0:T(8,128)S(1)}, u32[]{:S(2)}) copy-start(s32[1,32,8]{2,1,0:T(8,128)S(1)} %copy.33) | copy-start | bytes 3076
  11.6 3.5 copy-start.16
  146.9 257.0 %copy-start.10 = (f32[64]{0:T(128)}, f32[64]{0:T(128)S(1)}, u32[]{:S(2)}) copy-start(f32[64]{0:T(128)S(1)} %psum.49) | copy-start | bytes 772
  147.0 256.9 %copy-start.11 = (f32[32]{0:T(128)}, f32[32]{0:T(128)S(1)}, u32[]{:S(2)}) copy-start(f32[32]{0:T(128)S(1)} %fusion.65) | copy-start | bytes 388
  271.2 132.7 %copy-start.12 = (f32[64]{0:T(128)}, f32[64]{0:T(128)S(1)}, u32[]{:S(2)}) copy-start(f32[64]{0:T(128)S(1)} %psum.50) | copy-start | bytes 772
  271.3 132.6 %copy-start.13 = (f32[32]{0:T(128)}, f32[32]{0:T(128)S(1)}, u32[]{:S(2)}) copy-start(f32[32]{0:T(128)S(1)} %fusion.70) | copy-start | bytes 388
  396.8 7.2 copy-start.21
  398.9 14.0 %all-to-all-start = ((bf16[64,1,8]{2,1,0:T(2,128)(2,1)}), bf16[64,1,8]{2,1,0:T(2,128)(2,1)S(1)}, u32[]{:S(2)}, u32[]{:S(2)}) async-start(bf16[64,1,8]{2,1,0:T(2,128)(2,1)} %all_to_all.25), calls=%async_computation | async-start | bytes 65536 | tf_op jit(solution)/shard_map/all_to_all | solution.py:105
  403.9 14.6 %copy-start.4 = (bf16[512,32]{0,1:T(8,128)(2,1)}, bf16[512,32]{0,1:T(8,128)(2,1)S(1)}, u32[]{:S(2)}) copy-start(bf16[512,32]{0,1:T(8,128)(2,1)S(1)} %fusion.41) | copy-start | bytes 98308
  406.9 11.7 copy-start.9
  413.0 56.6 %all-to-all-start.2 = ((bf16[64,8,2048]{2,1,0:T(8,128)(2,1)}), bf16[64,8,2048]{2,1,0:T(8,128)(2,1)}, u32[]{:S(2)}, u32[]{:S(2)}) async-start(bf16[64,8,2048]{2,1,0:T(8,128)(2,1)} %fusion.13), calls=%async_computation.2 | async-start | bytes 4194304 | tf_op jit(solution)/shard_map/all_to_all | solution.py:91
  469.6 57.2 %all-to-all-start.1 = ((bf16[64,8,2048]{2,1,0:T(8,128)(2,1)}), bf16[64,8,2048]{2,1,0:T(8,128)(2,1)}, u32[]{:S(2)}, u32[]{:S(2)}) async-start(bf16[64,8,2048]{2,1,0:T(8,128)(2,1)} %fusion.12), calls=%async_computation.1 | async-start | bytes 4194304 | tf_op jit(solution)/shard_map/all_to_all | solution.py:98
  475.7 525.0 %reduce-scatter.2.cloned.1.call-start = ((), (), s32[]{:S(2)}) async-start(), calls=%async_computation.7 | async-start | bytes 11796480 | tf_op jit(solution)/shard_map/reduce_scatter | solution.py:137
  526.7 4.6 copy-start.27
  526.7 4.7 copy-start.32
  526.7 4.7 copy-start.33
  535.4 4.0 copy-start.29
  535.4 4.0 copy-start.31
  548.1 15.4 %all-to-all-start.4 = ((bf16[64,1,8]{2,1,0:T(2,128)(2,1)}), bf16[64,1,8]{2,1,0:T(2,128)(2,1)}, u32[]{:S(2)}, u32[]{:S(2)}) async-start(bf16[64,1,8]{2,1,0:T(2,128)(2,1)} %convert_element_type.108), calls=%async_computation.4 | async-start | bytes 65536 | tf_op jit(solution)/shard_map/all_to_all | solution.py:123
  560.9 433.5 %copy-start.1 = (bf16[2048,64]{0,1:T(8,128)(2,1)S(1)}, bf16[2048,64]{0,1:T(8,128)(2,1)}, u32[]{:S(2)}) copy-start(bf16[2048,64]{0,1:T(8,128)(2,1)} %param.10) | copy-start | bytes 786436
  560.9 433.5 %copy-start.2 = (bf16[1,32,2048]{2,1,0:T(8,128)(2,1)S(1)}, bf16[1,32,2048]{2,1,0:T(8,128)(2,1)}, u32[]{:S(2)}) copy-start(bf16[1,32,2048]{2,1,0:T(8,128)(2,1)} %param.7) | copy-start | bytes 393220
  563.5 434.1 %all-to-all-start.3 = ((bf16[64,8,2048]{2,1,0:T(8,128)(2,1)}), bf16[64,8,2048]{2,1,0:T(8,128)(2,1)}, u32[]{:S(2)}, u32[]{:S(2)}) async-start(bf16[64,8,2048]{2,1,0:T(8,128)(2,1)} %fusion.14), calls=%async_computation.3 | async-start | bytes 4194304 | tf_op jit(solution)/shard_map/all_to_all | solution.py:116
  571.2 670.8 %all-reduce.2.cloned.1.call-start = ((), (), s32[]{:S(2)}) async-start(), calls=%async_computation.6 | async-start | bytes 1048576 | tf_op jit(solution)/shard_map/psum | solution.py:170
  (17 other events, 26.2 us)
Sparse Core Ops, SparseCore 0:
  547.5 87.0 reduce-scatter.1
Sparse Core Ops, SparseCore 1:
  996.5 245.4 all-reduce.1
where the time goes:
time: 1250 us
  blocking collectives  785 us (63%)
  waiting for transfers between devices  330 us (26%)
  matrix products  46 us (4%)
  starting transfers between devices  30.6 us (2%)
  other arithmetic  24.4 us (2%)
  local copies, waits for them, and re-layouts  19.8 us (2%)
  between operations  16 us (1%)
    psum x3, blocking collectives, per_device(): moment = lax.psum(jnp.sum(scaled_grad * scaled, axis=0), 'ep')  405 us
    psum x3, blocking collectives, column_sums(): return lax.psum(jnp.sum(values, axis=0), 'ep')  380 us
    psum x1, waiting for transfers between devices, per_device(): grad_router = lax.psum(router_part, ('dp', 'ep'))  231 us
    all_to_all x1, waiting for transfers between devices, per_device(): lax.all_to_all(send_tokens.reshape(experts, slot_cap, model_width), 'ep',...  49 us
    all_to_all x1, waiting for transfers between devices, per_device(): lax.all_to_all(send_cotangent.reshape(experts, slot_cap, model_width), 'e...  40.5 us
  transfers between devices with their start and end apart: 7, of which 5 were waited for; matrix products, arithmetic and copies ran while one was open for 4% of the time, Pallas kernels for 0%

commit v1 on v0

--- a/solution.py
+++ b/solution.py
@@ -163,7 +163,8 @@
         scaled_grad = (
             kernel_grad - jnp.sum(kernel_grad * kernel_step, axis=1, keepdims=True)
         ) / row_total
-        moment = lax.psum(jnp.sum(scaled_grad * scaled, axis=0), "ep")
+        sample = jnp.sum(scaled_grad * scaled, axis=0)
+        moment = jnp.sum(jax.lax.all_gather(sample, "ep"), axis=0)
         kernel_grad = (scaled_grad - moment[None, :]) / column[None, :]
     logit_grad = kernel_grad * kernel_start
     router_back, router_part = logit_vjp(logit_grad)

time: 1250 us -> 1630 us (1.30)
  blocking collectives: 785 us -> 1150 us
    unnamed x0 -> x3, blocking collectives: none -> 766 us
    psum x3 -> x0, blocking collectives: 405 us -> none  [per_device(): moment = lax.psum(jnp.sum(scaled_grad * scaled, axis=0), 'ep')]
where the time goes in v1:
time: 1630 us
  blocking collectives  1150 us (71%)
  waiting for transfers between devices  330 us (20%)
  matrix products  46 us (3%)
  local copies, waits for them, and re-layouts  31 us (2%)
  starting transfers between devices  30.6 us (2%)
  other arithmetic  28.3 us (2%)
  between operations  16.6 us (1%)
    unnamed x3, blocking collectives  766 us
    psum x3, blocking collectives, column_sums(): return lax.psum(jnp.sum(values, axis=0), 'ep')  380 us
    psum x1, waiting for transfers between devices, per_device(): grad_router = lax.psum(router_part, ('dp', 'ep'))  231 us
    all_to_all x1, waiting for transfers between devices, per_device(): lax.all_to_all(send_tokens.reshape(experts, slot_cap, model_width), 'ep',...  49 us
    all_to_all x1, waiting for transfers between devices, per_device(): lax.all_to_all(send_cotangent.reshape(experts, slot_cap, model_width), 'e...  40.5 us
  transfers between devices with their start and end apart: 7, of which 5 were waited for; matrix products, arithmetic and copies ran while one was open for 4% of the time, Pallas kernels for 0%

profile of v1, /device:TPU:2, one launch (start us, length us, event | category | flops | bytes accessed | tf_op | source)
XLA Modules:
  0.0 1628.1 jit_solution(1117943553563010411)
XLA Ops:
  15.1 131.8 %psum.28 = f32[64]{0:T(128)S(1)} all-reduce(f32[64]{0:T(128)S(1)} %get-tuple-element.33), channel_id=1, replica_groups=mesh['dp'=4,'ep'=64] {'ep'}, use_global_device_ids=true, to_apply=%region_7.0 | all-reduce | flops 64 | bytes 512 | tf_op jit(solution)/shard_map/psum | solution.py:43
  147.1 124.1 %psum.29 = f32[64]{0:T(128)S(1)} all-reduce(f32[64]{0:T(128)S(1)} %fusion.67), channel_id=1, replica_groups=mesh['dp'=4,'ep'=64] {'ep'}, use_global_device_ids=true, to_apply=%region_10.0 | all-reduce | flops 64 | bytes 512 | tf_op jit(solution)/shard_map/psum | solution.py:43
  271.4 124.0 %psum.30 = f32[64]{0:T(128)S(1)} all-reduce(f32[64]{0:T(128)S(1)} %fusion.73), channel_id=1, replica_groups=mesh['dp'=4,'ep'=64] {'ep'}, use_global_device_ids=true, to_apply=%region_13.0 | all-reduce | flops 64 | bytes 512 | tf_op jit(solution)/shard_map/psum | solution.py:43
  398.9 4.6 all-to-all-start
  406.9 6.1 all-to-all-done
  413.0 5.6 all-to-all-start.2
  420.6 49.0 %all-to-all-done.2 = bf16[64,8,2048]{2,1,0:T(8,128)(2,1)} async-done(((bf16[64,8,2048]{2,1,0:T(8,128)(2,1)}), bf16[64,8,2048]{2,1,0:T(8,128)(2,1)}, u32[]{:S(2)}, u32[]{:S(2)}) %all-to-all-start.2) | async-done | bytes 2097184 | tf_op jit(solution)/shard_map/all_to_all | solution.py:91
  469.6 6.1 all-to-all-start.1
  476.1 5.5 fusion.6
  481.6 4.6 fusion.2
  486.2 40.5 %all-to-all-done.1 = bf16[64,8,2048]{2,1,0:T(8,128)(2,1)} async-done(((bf16[64,8,2048]{2,1,0:T(8,128)(2,1)}), bf16[64,8,2048]{2,1,0:T(8,128)(2,1)}, u32[]{:S(2)}, u32[]{:S(2)}) %all-to-all-start.1) | async-done | bytes 2097184 | tf_op jit(solution)/shard_map/all_to_all | solution.py:98
  526.7 4.6 convolution_convert_fusion
  531.4 4.0 multiply_reduce_fusion
  535.4 4.0 convolution_convert_fusion.1
  539.5 3.4 convolution_convert_fusion.2
  542.9 4.5 pad_maximum_fusion
  548.1 6.4 all-to-all-start.4
  554.5 3.3 fusion
  557.8 3.1 fusion.14
  563.5 7.7 all-to-all-start.3
  584.3 273.9 %all-reduce = f32[4096]{0:T(1024)} all-reduce(f32[4096]{0:T(1024)} %dynamic-update-slice), channel_id=2, replica_groups=mesh['dp'=4,'ep'=64] {'ep'}, use_global_device_ids=true, to_apply=%add | all-reduce | flops 4096 | bytes 32768
  865.8 246.1 %all-reduce.1 = f32[4096]{0:T(1024)} all-reduce(f32[4096]{0:T(1024)} %dynamic-update-slice.1), channel_id=3, replica_groups=mesh['dp'=4,'ep'=64] {'ep'}, use_global_device_ids=true, to_apply=%add.1 | all-reduce | flops 4096 | bytes 32768
  1119.5 246.1 %all-reduce.2 = f32[4096]{0:T(1024)} all-reduce(f32[4096]{0:T(1024)} %dynamic-update-slice.2), channel_id=4, replica_groups=mesh['dp'=4,'ep'=64] {'ep'}, use_global_device_ids=true, to_apply=%add.2 | all-reduce | flops 4096 | bytes 32768
  1387.5 231.3 %all-reduce.5.cloned.1.call-done = f32[2048,64]{0,1:T(8,128)} async-done(((f32[2048,64]{0,1:T(8,128)}), f32[2048,64]{0,1:T(8,128)}) %all-reduce.5.cloned.1.call-update) | async-done | bytes 524304 | tf_op jit(solution)/shard_map/psum | solution.py:171
  (147 shorter events, 71.2 us)
Async XLA Ops:
  8.0 473.6 %copy-start = (bf16[1,2048,768]{2,1,0:T(8,128)(2,1)S(1)}, bf16[1,2048,768]{2,1,0:T(8,128)(2,1)}, u32[]{:S(2)}) copy-start(bf16[1,2048,768]{2,1,0:T(8,128)(2,1)} %param.11) | copy-start | bytes 9437188
  8.9 404.0 %copy-start.3 = (s32[1,32,8]{2,1,0:T(8,128)}, s32[1,32,8]{2,1,0:T(8,128)S(1)}, u32[]{:S(2)}) copy-start(s32[1,32,8]{2,1,0:T(8,128)S(1)} %copy.33) | copy-start | bytes 3076
  11.6 3.5 copy-start.16
  146.9 257.0 %copy-start.10 = (f32[64]{0:T(128)}, f32[64]{0:T(128)S(1)}, u32[]{:S(2)}) copy-start(f32[64]{0:T(128)S(1)} %psum.28) | copy-start | bytes 772
  147.0 256.9 %copy-start.11 = (f32[32]{0:T(128)}, f32[32]{0:T(128)S(1)}, u32[]{:S(2)}) copy-start(f32[32]{0:T(128)S(1)} %fusion.65) | copy-start | bytes 388
  271.2 132.7 %copy-start.12 = (f32[64]{0:T(128)}, f32[64]{0:T(128)S(1)}, u32[]{:S(2)}) copy-start(f32[64]{0:T(128)S(1)} %psum.29) | copy-start | bytes 772
  271.3 132.6 %copy-start.13 = (f32[32]{0:T(128)}, f32[32]{0:T(128)S(1)}, u32[]{:S(2)}) copy-start(f32[32]{0:T(128)S(1)} %fusion.70) | copy-start | bytes 388
  396.8 7.2 copy-start.21
  398.9 14.0 all-to-all-start
  403.9 14.6 copy-start.4
  406.9 11.7 copy-start.9
  413.0 56.6 %all-to-all-start.2 = ((bf16[64,8,2048]{2,1,0:T(8,128)(2,1)}), bf16[64,8,2048]{2,1,0:T(8,128)(2,1)}, u32[]{:S(2)}, u32[]{:S(2)}) async-start(bf16[64,8,2048]{2,1,0:T(8,128)(2,1)} %fusion.13), calls=%async_computation.2 | async-start | bytes 4194304 | tf_op jit(solution)/shard_map/all_to_all | solution.py:91
  469.6 57.2 %all-to-all-start.1 = ((bf16[64,8,2048]{2,1,0:T(8,128)(2,1)}), bf16[64,8,2048]{2,1,0:T(8,128)(2,1)}, u32[]{:S(2)}, u32[]{:S(2)}) async-start(bf16[64,8,2048]{2,1,0:T(8,128)(2,1)} %fusion.12), calls=%async_computation.1 | async-start | bytes 4194304 | tf_op jit(solution)/shard_map/all_to_all | solution.py:98
  475.7 901.8 %reduce-scatter.2.cloned.1.call-start = ((), (), s32[]{:S(2)}) async-start(), calls=%async_computation.7 | async-start | bytes 11796480 | tf_op jit(solution)/shard_map/reduce_scatter | solution.py:137
  526.7 4.6 copy-start.27
  526.7 4.7 copy-start.32
  526.7 4.7 copy-start.33
  535.4 4.0 copy-start.29
  535.4 4.0 copy-start.31
  548.1 15.4 all-to-all-start.4
  560.9 810.3 %copy-start.1 = (bf16[2048,64]{0,1:T(8,128)(2,1)S(1)}, bf16[2048,64]{0,1:T(8,128)(2,1)}, u32[]{:S(2)}) copy-start(bf16[2048,64]{0,1:T(8,128)(2,1)} %param.10) | copy-start | bytes 786436
  560.9 810.3 %copy-start.2 = (bf16[1,32,2048]{2,1,0:T(8,128)(2,1)S(1)}, bf16[1,32,2048]{2,1,0:T(8,128)(2,1)}, u32[]{:S(2)}) copy-start(bf16[1,32,2048]{2,1,0:T(8,128)(2,1)} %param.7) | copy-start | bytes 393220
  563.5 810.8 %all-to-all-start.3 = ((bf16[64,8,2048]{2,1,0:T(8,128)(2,1)}), bf16[64,8,2048]{2,1,0:T(8,128)(2,1)}, u32[]{:S(2)}, u32[]{:S(2)}) async-start(bf16[64,8,2048]{2,1,0:T(8,128)(2,1)} %fusion.14), calls=%async_computation.3 | async-start | bytes 4194304 | tf_op jit(solution)/shard_map/all_to_all | solution.py:116
  571.2 1047.5 %all-reduce.5.cloned.1.call-start = ((), (), s32[]{:S(2)}) async-start(), calls=%async_computation.6 | async-start | bytes 1048576 | tf_op jit(solution)/shard_map/psum | solution.py:171
  (17 other events, 27.0 us)
Sparse Core Ops, SparseCore 0:
  547.5 87.0 reduce-scatter.1
Sparse Core Ops, SparseCore 1:
  1373.3 245.4 all-reduce.4
